TPU v7x, 512 devices: a whole 4x8x8 slice. The times are simulated.
512 devices in a mesh: lat: 64 (over z, y), batch: 8 (over x, core).
Axes of the slice: x: 4, y: 8, z: 8, core: 2. Of those that a mesh axis runs over, the one named last changes fastest.
Arguments:
- fields: bfloat16 [8, 192, 384, 384], P('batch', 'lat'), may hold values from -6 to 6
- cotangent: bfloat16 [8, 192, 384, 384], P('batch', 'lat'), may hold values from -6 to 6
- weights: bfloat16 [128, 2, 384, 384], P('lat'), may hold values from -0.21875 to 0.21875
- degree_of: int32 [128], replicated, may hold values from 0 to 127, each once
Outputs:
- grad_fields: bfloat16 [8, 192, 384, 384], P('batch', 'lat')
- grad_weights: bfloat16 [128, 2, 384, 384], P('lat')
Inputs may be any that keep to these rules, and one draw needn't show every extreme that they name: `degree_of`: each degree 0 to 127 is held by exactly one slot.
All inputs are finite; a program needn't handle non-finite values.
Results may differ from a plain program's by a relative error of at most 0.018.
Values may be sent and summed in bfloat16 or wider, within the bound.
No kernel may reach another device: no remote copies, remote signals or barrier semaphores. Data moves between devices by JAX's collectives and lax.ppermute only.
A program may use at most 64 MiB of HBM per device.

v0:
```python
import jax
import jax.numpy as jnp
from jax import lax
from jax.sharding import PartitionSpec as P

LATS = 192
LONS = 384
ORDERS = 128
DEGREES = 128
CHANNELS = 384


def in_one_piece(arrays, axis, dim, along):
    widths = [a.shape[along] for a in arrays]
    both = jnp.concatenate(arrays, axis=along)
    out = lax.all_gather(both, axis, axis=dim, tiled=True)
    return tuple(jnp.split(out, [sum(widths[:k]) for k in range(1, len(widths))], axis=along))


def legendre_table(order_ids, lat_count, degree_count):
    colatitude = jnp.pi * (jnp.arange(lat_count, dtype=jnp.float32) + 0.5) / lat_count
    cosine = jnp.cos(colatitude)[None, :]
    log_sine = jnp.log(jnp.sin(colatitude))[None, :]
    order_col = order_ids[:, None]
    order_real = order_col.astype(jnp.float32)
    steps_up = jnp.arange(1, degree_count + 1, dtype=jnp.float32)[None, :]
    factor = jnp.where(
        steps_up <= order_real, 0.5 * jnp.log((2.0 * steps_up + 1.0) / (2.0 * steps_up)), 0.0
    )
    log_start = 0.5 * jnp.log(1.0 / (4.0 * jnp.pi)) + jnp.sum(factor, axis=1, keepdims=True)
    diagonal = jnp.exp(log_start + order_real * log_sine)
    squared = order_real * order_real

    def advance(carry, degree):
        previous, older = carry
        degree_real = degree.astype(jnp.float32)
        lead = jnp.sqrt(
            jnp.maximum(4.0 * degree_real * degree_real - 1.0, 0.0)
            / jnp.maximum(degree_real * degree_real - squared, 1.0)
        )
        lower = degree_real - 1.0
        back = jnp.sqrt(
            jnp.maximum(lower * lower - squared, 0.0) / jnp.maximum(4.0 * lower * lower - 1.0, 1.0)
        )
        general = lead * (cosine * previous - back * older)
        first = jnp.sqrt(2.0 * order_real + 3.0) * cosine * previous
        value = jnp.where(
            degree == order_col,
            diagonal,
            jnp.where(
                degree == order_col + 1, first, jnp.where(degree > order_col + 1, general, 0.0)
            ),
        )
        return ((value, previous), value)

    zeros = jnp.zeros((order_ids.shape[0], lat_count), jnp.float32)
    final_state, table = lax.scan(
        advance, (zeros, zeros), jnp.arange(degree_count, dtype=jnp.int32)
    )
    return jnp.transpose(table, (1, 0, 2))


def spectral_tables(start, ord_dev, degree_of):
    order_ids = start + jnp.arange(ord_dev, dtype=jnp.int32)
    mine = legendre_table(order_ids, LATS, DEGREES)
    selector = (degree_of[:, None] == jnp.arange(DEGREES, dtype=jnp.int32)[None, :]).astype(
        jnp.float32
    )
    chosen = jnp.einsum("mli,jl->mji", mine, selector, precision=lax.Precision.HIGHEST)
    colatitude = jnp.pi * (jnp.arange(LATS, dtype=jnp.float32) + 0.5) / LATS
    quadrature = 2.0 * jnp.pi * jnp.pi / LATS * jnp.sin(colatitude)
    return ((chosen * quadrature[None, None, :]).astype(jnp.bfloat16), chosen.astype(jnp.bfloat16))


def fourier_tables(lon_count, order_count):
    lon_ids = jnp.arange(lon_count, dtype=jnp.int32)[:, None]
    order_ids = jnp.arange(order_count, dtype=jnp.int32)[None, :]
    phase = 2.0 * jnp.pi * (lon_ids * order_ids % lon_count).astype(jnp.float32) / lon_count
    forward = (
        jnp.stack([jnp.cos(phase), -jnp.sin(phase)], axis=2).reshape(lon_count, 2 * order_count)
        / lon_count
    )
    doubled = jnp.where(order_ids == 0, 1.0, 2.0)
    inverse = jnp.stack([doubled * jnp.cos(phase), -doubled * jnp.sin(phase)], axis=2).reshape(
        lon_count, 2 * order_count
    )
    return (forward.astype(jnp.bfloat16), jnp.transpose(inverse).astype(jnp.bfloat16))


def to_orders(values):
    return lax.all_to_all(values, "lat", split_axis=1, concat_axis=0, tiled=True)


def to_degrees(values):
    return lax.all_to_all(values, "lat", split_axis=0, concat_axis=1, tiled=True)


def back_to_orders(values):
    return lax.all_to_all(values, "lat", split_axis=1, concat_axis=0, tiled=True)


def to_bands(values):
    return lax.all_to_all(values, "lat", split_axis=0, concat_axis=1, tiled=True)


def product(spec, left, right):
    return jnp.einsum(spec, left, right, preferred_element_type=jnp.float32)


def apply_filter(coeffs, weights):
    c_real = coeffs[:, :, 0]
    c_imag = coeffs[:, :, 1]
    w_real = weights[:, 0]
    w_imag = weights[:, 1]
    f_real = product("jmsc,jcd->jmsd", c_real, w_real) - product("jmsc,jcd->jmsd", c_imag, w_imag)
    f_imag = product("jmsc,jcd->jmsd", c_real, w_imag) + product("jmsc,jcd->jmsd", c_imag, w_real)
    return jnp.stack([f_real, f_imag], axis=2).astype(jnp.bfloat16)


def adjoint_filter(grads, weights):
    g_real = grads[:, :, 0]
    g_imag = grads[:, :, 1]
    w_real = weights[:, 0]
    w_imag = weights[:, 1]
    a_real = product("jmsd,jcd->jmsc", g_real, w_real) + product("jmsd,jcd->jmsc", g_imag, w_imag)
    a_imag = product("jmsd,jcd->jmsc", g_imag, w_real) - product("jmsd,jcd->jmsc", g_real, w_imag)
    return jnp.stack([a_real, a_imag], axis=2).astype(jnp.bfloat16)


def filter_grad(coeffs, grads):
    c_real = coeffs[:, :, 0]
    c_imag = coeffs[:, :, 1]
    g_real = grads[:, :, 0]
    g_imag = grads[:, :, 1]
    dw_real = product("jmsc,jmsd->jcd", c_real, g_real) + product("jmsc,jmsd->jcd", c_imag, g_imag)
    dw_imag = product("jmsc,jmsd->jcd", c_real, g_imag) - product("jmsc,jmsd->jcd", c_imag, g_real)
    return jnp.stack([dw_real, dw_imag], axis=1)


def local(fields, cotangent, weights, degree_of):
    samples = fields.shape[0]
    band_rows = fields.shape[1]
    ord_dev = ORDERS // lax.axis_size("lat")
    forward, inverse = fourier_tables(LONS, ORDERS)
    qslot, pslot = spectral_tables(lax.axis_index("lat") * ord_dev, ord_dev, degree_of)
    spectra = product("sikc,kf->ifsc", fields, forward).astype(jnp.bfloat16)
    spectra = spectra.reshape(band_rows, ORDERS, 2, samples, CHANNELS)
    gathered = to_orders(spectra)
    coeffs_local = product("mji,imrsc->jmrsc", qslot, gathered).astype(jnp.bfloat16)
    coeffs = to_degrees(coeffs_local)
    filtered = apply_filter(coeffs, weights)
    returned = back_to_orders(filtered)
    synth_local = product("mji,jmrsc->imrsc", pslot, returned).astype(jnp.bfloat16)
    synth = to_bands(synth_local)
    response = product(
        "ifsc,fk->sikc", synth.reshape(band_rows, 2 * ORDERS, samples, CHANNELS), inverse
    )
    activated, pullback = jax.vjp(jax.nn.gelu, response)
    upstream = pullback(cotangent.astype(jnp.float32))[0].astype(jnp.bfloat16)
    grad_synth = product("sikc,fk->ifsc", upstream, inverse).astype(jnp.bfloat16)
    grad_synth = grad_synth.reshape(band_rows, ORDERS, 2, samples, CHANNELS)
    grad_gathered = to_orders(grad_synth)
    grad_local = product("mji,imrsc->jmrsc", pslot, grad_gathered).astype(jnp.bfloat16)
    grad_filtered = to_degrees(grad_local)
    all_coeffs, all_grads = in_one_piece((coeffs, grad_filtered), "batch", 3, 0)
    weight_total = filter_grad(all_coeffs, all_grads)
    grad_coeffs = adjoint_filter(grad_filtered, weights)
    grad_back = back_to_orders(grad_coeffs)
    grad_local_spec = product("mji,jmrsc->imrsc", qslot, grad_back).astype(jnp.bfloat16)
    grad_bands = to_bands(grad_local_spec)
    delta = product(
        "ifsc,kf->sikc", grad_bands.reshape(band_rows, 2 * ORDERS, samples, CHANNELS), forward
    )
    grad_fields = (cotangent.astype(jnp.float32) + delta).astype(jnp.bfloat16)
    return (grad_fields, weight_total.astype(jnp.bfloat16))


def solution(mesh):
    return jax.shard_map(
        local,
        mesh=mesh,
        in_specs=(
            P("batch", "lat", None, None),
            P("batch", "lat", None, None),
            P("lat", None, None, None),
            P(),
        ),
        out_specs=(P("batch", "lat", None, None), P("lat", None, None, None)),
        check_vma=False,
    )
```

profile of v0, /device:TPU:6, one launch (start us, length us, event | category | flops | bytes accessed | tf_op | source)
XLA Modules:
  0.0 588.7 jit_solution(4414124567485048653)
XLA Ops:
  9.7 1.2 copy.172
  11.0 16.6 %all-to-all-start = ((bf16[3,128,2,1,384]{4,2,0,3,1:T(2,128)(2,1)}), bf16[3,128,2,1,384]{4,2,0,3,1:T(2,128)(2,1)S(1)}, u32[]{:S(2)}, u32[]{:S(2)}) async-start(bf16[3,128,2,1,384]{4,2,0,3,1:T(2,128)(2,1)} %copy.172), calls=%async_computation | async-start | bytes 1179648 | tf_op jit(solution)/shard_map/all_to_all | solution.py:91
  27.9 350.0 %while.21 = (s32[]{:T(128)}, f32[2,192]{1,0:T(2,128)S(1)}, f32[2,192]{1,0:T(2,128)S(1)}, f32[128,2,192]{2,1,0:T(2,128)S(1)}, s32[128]{0:T(128)S(1)}, /*index=5*/...) while((s32[]{:T(128)}, f32[2,192]{1,0:T(2,128)S(1)}, ...), condition=%wide.region_2.3_spmd.clone.clone.clone.clone, body=%wide.region_1.2_spmd.clone.clone.clone.clone.sunk | while | flops 5047 | bytes 17529 | solution.py:57
  379.3 1.3 fusion.38
  380.6 1.4 copy.177
  382.0 29.2 %all_to_all.126 = bf16[128,2,2,1,384]{4,2,1,3,0:T(2,128)(2,1)S(1)} all-to-all(bf16[128,2,2,1,384]{4,2,1,3,0:T(2,128)(2,1)S(1)} %copy.177), channel_id=1, replica_groups=mesh['lat'=64,'batch'=8] {'lat'}, dimensions={0} | all-to-all | bytes 786432 | tf_op jit(solution)/shard_map/all_to_all | solution.py:95
  413.3 20.7 %all_to_all.127 = bf16[2,128,2,1,384]{4,0,3,2,1:T(2,128)(2,1)S(1)} all-to-all(bf16[2,128,2,1,384]{4,0,3,2,1:T(2,128)(2,1)S(1)} %copy.181), channel_id=1, replica_groups=mesh['lat'=64,'batch'=8] {'lat'}, dimensions={1} | all-to-all | bytes 786432 | tf_op jit(solution)/shard_map/all_to_all | solution.py:99
  435.2 1.3 fusion.32
  436.5 1.4 copy.183
  437.9 5.5 all-to-all-start.3
  446.2 16.2 %all-to-all-done.3 = bf16[192,2,2,1,384]{4,2,1,3,0:T(2,128)(2,1)} async-done(((bf16[192,2,2,1,384]{4,2,1,3,0:T(2,128)(2,1)}), bf16[192,2,2,1,384]{4,2,1,3,0:T(2,128)(2,1)}, u32[]{:S(2)}, u32[]{:S(2)}) %all-to-all-start.3) | async-done | bytes 589856 | tf_op jit(solution)/shard_map/all_to_all | solution.py:103
  462.4 1.5 copy.184
  463.9 1.0 reshape.469
  464.9 4.0 fusion.36
  468.9 1.9 reshape.471
  471.2 24.4 %all_to_all.128 = bf16[3,128,2,1,384]{4,2,0,3,1:T(2,128)(2,1)S(1)} all-to-all(bf16[3,128,2,1,384]{4,2,0,3,1:T(2,128)(2,1)S(1)} %copy.186), channel_id=1, replica_groups=mesh['lat'=64,'batch'=8] {'lat'}, dimensions={1} | all-to-all | bytes 1179648 | tf_op jit(solution)/shard_map/all_to_all | solution.py:91
  496.4 1.2 fusion.39
  497.6 1.3 copy.190
  498.9 20.7 %all_to_all.129 = bf16[128,2,2,1,384]{4,2,1,3,0:T(2,128)(2,1)S(1)} all-to-all(bf16[128,2,2,1,384]{4,2,1,3,0:T(2,128)(2,1)S(1)} %copy.190), channel_id=1, replica_groups=mesh['lat'=64,'batch'=8] {'lat'}, dimensions={0} | all-to-all | bytes 786432 | tf_op jit(solution)/shard_map/all_to_all | solution.py:95
  519.7 1.0 copy.191
  520.7 1.1 all_to_all.111
  521.9 1.0 pad_maximum_fusion.1
  524.6 19.7 %all_to_all.130 = bf16[2,128,2,1,384]{4,0,3,2,1:T(2,128)(2,1)S(1)} all-to-all(bf16[2,128,2,1,384]{4,0,3,2,1:T(2,128)(2,1)S(1)} %copy.192), channel_id=1, replica_groups=mesh['lat'=64,'batch'=8] {'lat'}, dimensions={1} | all-to-all | bytes 786432 | tf_op jit(solution)/shard_map/all_to_all | solution.py:99
  545.1 1.4 copy.194
  546.5 4.6 all-to-all-start.7
  551.3 18.0 %all-to-all-done.7 = bf16[192,2,2,1,384]{4,2,1,3,0:T(2,128)(2,1)S(1)} async-done(((bf16[192,2,2,1,384]{4,2,1,3,0:T(2,128)(2,1)}), bf16[192,2,2,1,384]{4,2,1,3,0:T(2,128)(2,1)S(1)}, u32[]{:S(2)}, u32[]{:S(2)}) %all-to-all-start.7) | async-done | bytes 589856 | tf_op jit(solution)/shard_map/all_to_all | solution.py:103
  570.0 2.6 fusion.24
  572.5 3.1 convolution_bitcast_fusion.2
  575.6 2.9 convolution_bitcast_fusion
  578.5 1.0 fusion.34
  579.6 1.0 fusion.35
  580.7 1.1 copy.201
  (967 shorter events, 277.0 us)
Async XLA Ops:
  7.2 1.8 copy-start
  8.3 0.7 copy-start.2
  9.7 368.4 %copy-start.5 = (s32[128]{0:T(128)S(1)}, s32[128]{0:T(128)}, u32[]{:S(2)}) copy-start(s32[128]{0:T(128)} %param.9) | copy-start | bytes 1540
  11.0 367.5 %all-to-all-start = ((bf16[3,128,2,1,384]{4,2,0,3,1:T(2,128)(2,1)}), bf16[3,128,2,1,384]{4,2,0,3,1:T(2,128)(2,1)S(1)}, u32[]{:S(2)}, u32[]{:S(2)}) async-start(bf16[3,128,2,1,384]{4,2,0,3,1:T(2,128)(2,1)} %copy.172), calls=%async_computation | async-start | bytes 1179648 | tf_op jit(solution)/shard_map/all_to_all | solution.py:91
  380.6 31.1 %copy-start.1 = (bf16[2,2,384,384]{3,2,1,0:T(8,128)(2,1)S(1)}, bf16[2,2,384,384]{3,2,1,0:T(8,128)(2,1)}, u32[]{:S(2)}) copy-start(bf16[2,2,384,384]{3,2,1,0:T(8,128)(2,1)} %param.8) | copy-start | bytes 3538948
  437.9 24.5 %all-to-all-start.3 = ((bf16[192,2,2,1,384]{4,2,1,3,0:T(2,128)(2,1)}), bf16[192,2,2,1,384]{4,2,1,3,0:T(2,128)(2,1)}, u32[]{:S(2)}, u32[]{:S(2)}) async-start(bf16[192,2,2,1,384]{4,2,1,3,0:T(2,128)(2,1)} %copy.183), calls=%async_computation.3 | async-start | bytes 1179648 | tf_op jit(solution)/shard_map/all_to_all | solution.py:103
  443.4 129.2 %all-gather.2.cloned.1.call-start = ((), (), s32[]{:S(2)}) async-start(), calls=%async_computation.8 | async-start | bytes 7077888 | tf_op jit(solution)/shard_map/all_gather | solution.py:16
  446.2 18.7 %copy-start.4 = (bf16[384,256]{0,1:T(8,128)(2,1)S(1)}, bf16[384,256]{0,1:T(8,128)(2,1)}, u32[]{:S(2)}) copy-start(bf16[384,256]{0,1:T(8,128)(2,1)} %convert_element_type.174) | copy-start | bytes 589828
  544.7 6.4 %copy-start.3 = (bf16[384,128,2]{0,2,1:T(2,128)(2,1)S(1)}, bf16[384,128,2]{0,2,1:T(2,128)(2,1)}, u32[]{:S(2)}) copy-start(bf16[384,128,2]{0,2,1:T(2,128)(2,1)} %copy-done.2) | copy-start | bytes 589828
  546.5 22.8 %all-to-all-start.7 = ((bf16[192,2,2,1,384]{4,2,1,3,0:T(2,128)(2,1)}), bf16[192,2,2,1,384]{4,2,1,3,0:T(2,128)(2,1)S(1)}, u32[]{:S(2)}, u32[]{:S(2)}) async-start(bf16[192,2,2,1,384]{4,2,1,3,0:T(2,128)(2,1)} %copy.194), calls=%async_computation.7 | async-start | bytes 1179648 | tf_op jit(solution)/shard_map/all_to_all | solution.py:103
  572.5 6.0 %copy-start.6 = (bf16[4,128,2,8,384]{4,1,0,3,2:T(8,128)(2,1)S(1)}, bf16[4,128,2,8,384]{4,1,0,3,2:T(8,128)(2,1)}, u32[]{:S(2)}) copy-start(bf16[4,128,2,8,384]{4,1,0,3,2:T(8,128)(2,1)} %all-gather.2.cloned.1.call-done) | copy-start | bytes 18874372
Sparse Core Ops, SparseCore 0:
  523.0 36.7 all-gather.1
where the time goes:
time: 595 us; the launch traced here: 589 us
  other arithmetic  189 us (32%)
  blocking collectives  115 us (19%)
  local copies, waits for them, and re-layouts  99.9 us (17%)
  loops' own time  87.7 us (15%)
  waiting for transfers between devices  34.3 us (6%)
  starting transfers between devices  26.9 us (5%)
  matrix products  21.9 us (4%)
  between operations  14.5 us (2%)
    another operation x1, loops' own time, legendre_table(): lax.scan(advance, (zeros, zeros), jnp.arange(degree_count, dtype=jnp.int32))  87.7 us
    gt x128, other arithmetic, advance(): degree > order_col + 1  81.7 us
    eq x128, other arithmetic, advance(): degree == order_col  80.8 us
    dynamic_slice x128, local copies, waits for them, and re-layouts, legendre_table(): lax.scan(advance, (zeros, zeros), jnp.arange(degree_count, dtype=jnp.int32))  76.7 us
    all_to_all x2, blocking collectives, to_degrees(): lax.all_to_all(values, 'lat', split_axis=0, concat_axis=1, tiled=True)  50 us
    all_to_all x2, blocking collectives, back_to_orders(): lax.all_to_all(values, 'lat', split_axis=1, concat_axis=0, tiled=True)  40.3 us
    all_to_all x2, waiting for transfers between devices, to_bands(): lax.all_to_all(values, 'lat', split_axis=0, concat_axis=1, tiled=True)  34.3 us
    all_to_all x1, blocking collectives, to_orders(): lax.all_to_all(values, 'lat', split_axis=1, concat_axis=0, tiled=True)  24.4 us
  transfers between devices with their start and end apart: 4, of which 2 were waited for; matrix products, arithmetic and copies ran while one was open for 46% of the time, Pallas kernels for 0%

commit v1 on v0

--- a/solution.py
+++ b/solution.py
@@ -96,7 +96,10 @@
 
 
 def back_to_orders(values):
-    return lax.all_to_all(values, "lat", split_axis=1, concat_axis=0, tiled=True)
+    return jnp.concatenate(
+        lax.all_to_all(jnp.stack(jnp.split(values, lax.axis_size("lat"), axis=1)), "lat", 0, 0),
+        axis=0,
+    )
 
 
 def to_bands(values):

time: 595 us -> 622 us (1.045)
  other arithmetic: 189 us -> 206 us
  loops' own time: 87.7 us -> 96.1 us
  local copies, waits for them, and re-layouts: 99.9 us -> 107 us
    eq x128, other arithmetic: 80.8 us -> 89.2 us  [advance(): degree == order_col]
    another operation x1, loops' own time: 87.7 us -> 96.1 us  [legendre_table(): lax.scan(advance, (zeros, zeros), jnp.arange(degree_count, dtype=jnp.int32))]
    gt x128, other arithmetic: 81.7 us -> 90.1 us  [advance(): degree > order_col + 1]
    dynamic_slice x128, local copies, waits for them, and re-layouts: 76.7 us -> 85 us  [legendre_table(): lax.scan(advance, (zeros, zeros), jnp.arange(degree_count, dtype=jnp.int32))]
  transfers between devices with their start and end apart: 4 -> 4, of which waited for: 2 -> 2; matrix products, arithmetic and copies ran while one was open for 46% -> 48% of each run, Pallas kernels for 0% -> 0%
where the time goes in v1:
time: 622 us; the launch traced here: 616 us
  other arithmetic  206 us (33%)
  blocking collectives  113 us (18%)
  local copies, waits for them, and re-layouts  107 us (17%)
  loops' own time  96.1 us (15%)
  waiting for transfers between devices  32.2 us (5%)
  starting transfers between devices  26.9 us (4%)
  matrix products  20.9 us (3%)
  between operations  15 us (2%)
    another operation x1, loops' own time, legendre_table(): lax.scan(advance, (zeros, zeros), jnp.arange(degree_count, dtype=jnp.int32))  96.1 us
    gt x128, other arithmetic, advance(): degree > order_col + 1  90.1 us
    eq x128, other arithmetic, advance(): degree == order_col  89.2 us
    dynamic_slice x128, local copies, waits for them, and re-layouts, legendre_table(): lax.scan(advance, (zeros, zeros), jnp.arange(degree_count, dtype=jnp.int32))  85 us
    all_to_all x2, blocking collectives, to_degrees(): lax.all_to_all(values, 'lat', split_axis=0, concat_axis=1, tiled=True)  49.2 us
    all_to_all x2, blocking collectives, back_to_orders(): lax.all_to_all(jnp.stack(jnp.split(values, lax.axis_size('lat'), axis=1))...  39.7 us
    all_to_all x2, waiting for transfers between devices, to_bands(): lax.all_to_all(values, 'lat', split_axis=0, concat_axis=1, tiled=True)  32.2 us
    all_to_all x1, blocking collectives, to_orders(): lax.all_to_all(values, 'lat', split_axis=1, concat_axis=0, tiled=True)  24 us
  transfers between devices with their start and end apart: 4, of which 2 were waited for; matrix products, arithmetic and copies ran while one was open for 48% of the time, Pallas kernels for 0%

profile of v1, /device:TPU:6, one launch (start us, length us, event | category | flops | bytes accessed | tf_op | source)
XLA Modules:
  0.0 616.4 jit_solution(14163232432339468117)
XLA Ops:
  9.1 1.2 copy.930
  10.3 16.6 %all-to-all-start = ((bf16[3,128,2,1,384]{4,2,0,3,1:T(2,128)(2,1)}), bf16[3,128,2,1,384]{4,2,0,3,1:T(2,128)(2,1)S(1)}, u32[]{:S(2)}, u32[]{:S(2)}) async-start(bf16[3,128,2,1,384]{4,2,0,3,1:T(2,128)(2,1)} %copy.930), calls=%async_computation | async-start | bytes 1179648 | tf_op jit(solution)/shard_map/all_to_all | solution.py:91
  27.2 383.5 %while.21 = (s32[]{:T(128)}, f32[2,192]{1,0:T(2,128)S(1)}, f32[2,192]{1,0:T(2,128)S(1)}, f32[128,2,192]{2,1,0:T(2,128)S(1)}, s32[128]{0:T(128)S(1)}, /*index=5*/...) while((s32[]{:T(128)}, f32[2,192]{1,0:T(2,128)S(1)}, ...), condition=%wide.region_2.3_spmd.clone.clone.clone.clone, body=%wide.region_1.2_spmd.clone.clone.clone.clone.sunk | while | flops 5047 | bytes 17529 | solution.py:57
  413.1 29.2 %all_to_all.106 = bf16[128,2,2,1,384]{4,2,1,3,0:T(2,128)(2,1)S(1)} all-to-all(bf16[128,2,2,1,384]{4,2,1,3,0:T(2,128)(2,1)S(1)} %copy.935), channel_id=1, replica_groups=mesh['lat'=64,'batch'=8] {'lat'}, dimensions={0} | all-to-all | bytes 786432 | tf_op jit(solution)/shard_map/all_to_all | solution.py:95
  445.3 20.7 %all_to_all.107 = bf16[64,2,2,2,1,384]{5,2,1,3,4,0:T(2,128)(2,1)S(1)} all-to-all(bf16[64,2,2,2,1,384]{5,2,1,3,4,0:T(2,128)(2,1)S(1)} %constant_dynamic-update-slice_fusion), channel_id=1, replica_groups=mesh['lat'=64,'batch'=8] {'lat'}, dimensions={0} | all-to-all | bytes 786432 | tf_op jit(solution)/shard_map/all_to_all | solution.py:100
  466.6 1.4 copy.1004
  468.0 5.6 all-to-all-start.3
  473.8 0.8 multiply_convert_fusion.1
  476.3 16.1 %all-to-all-done.3 = bf16[192,2,2,1,384]{4,2,1,3,0:T(2,128)(2,1)} async-done(((bf16[192,2,2,1,384]{4,2,1,3,0:T(2,128)(2,1)}), bf16[192,2,2,1,384]{4,2,1,3,0:T(2,128)(2,1)}, u32[]{:S(2)}, u32[]{:S(2)}) %all-to-all-start.3) | async-done | bytes 589856 | tf_op jit(solution)/shard_map/all_to_all | solution.py:106
  492.5 1.5 copy.1005
  494.0 1.0 reshape.471
  495.0 4.1 fusion.36
  499.1 1.9 reshape.473
  501.4 24.0 %all_to_all.108 = bf16[3,128,2,1,384]{4,2,0,3,1:T(2,128)(2,1)S(1)} all-to-all(bf16[3,128,2,1,384]{4,2,0,3,1:T(2,128)(2,1)S(1)} %copy.1007), channel_id=1, replica_groups=mesh['lat'=64,'batch'=8] {'lat'}, dimensions={1} | all-to-all | bytes 1179648 | tf_op jit(solution)/shard_map/all_to_all | solution.py:91
  526.2 1.2 fusion.39
  527.4 1.3 copy.1011
  528.8 19.9 %all_to_all.109 = bf16[128,2,2,1,384]{4,2,1,3,0:T(2,128)(2,1)S(1)} all-to-all(bf16[128,2,2,1,384]{4,2,1,3,0:T(2,128)(2,1)S(1)} %copy.1011), channel_id=1, replica_groups=mesh['lat'=64,'batch'=8] {'lat'}, dimensions={0} | all-to-all | bytes 786432 | tf_op jit(solution)/shard_map/all_to_all | solution.py:95
  548.7 1.0 copy.1012
  549.7 1.1 all_to_all.93
  550.9 1.0 pad_maximum_fusion.1
  551.8 1.1 fusion.62
  553.3 1.3 fusion.45
  556.3 19.0 %all_to_all.110 = bf16[64,2,2,2,1,384]{5,2,1,3,4,0:T(2,128)(2,1)S(1)} all-to-all(bf16[64,2,2,2,1,384]{5,2,1,3,4,0:T(2,128)(2,1)S(1)} %constant_dynamic-update-slice_fusion.64), channel_id=1, replica_groups=mesh['lat'=64,'batch'=8] {'lat'}, dimensions={0} | all-to-all | bytes 786432 | tf_op jit(solution)/shard_map/all_to_all | solution.py:100
  576.0 1.4 copy.1078
  577.4 4.6 all-to-all-start.7
  582.1 16.1 %all-to-all-done.7 = bf16[192,2,2,1,384]{4,2,1,3,0:T(2,128)(2,1)S(1)} async-done(((bf16[192,2,2,1,384]{4,2,1,3,0:T(2,128)(2,1)}), bf16[192,2,2,1,384]{4,2,1,3,0:T(2,128)(2,1)S(1)}, u32[]{:S(2)}, u32[]{:S(2)}) %all-to-all-start.7) | async-done | bytes 589856 | tf_op jit(solution)/shard_map/all_to_all | solution.py:106
  598.9 1.4 fusion.24
  600.3 3.1 convolution_bitcast_fusion.2
  603.3 2.9 convolution_bitcast_fusion
  606.2 1.0 fusion.34
  607.3 1.0 fusion.35
  608.5 1.1 copy.1085
  (1087 shorter events, 301.4 us)
Async XLA Ops:
  7.2 1.2 copy-start
  9.1 401.9 %copy-start.3 = (s32[128]{0:T(128)S(1)}, s32[128]{0:T(128)}, u32[]{:S(2)}) copy-start(s32[128]{0:T(128)} %param.9) | copy-start | bytes 1540
  10.3 401.0 %all-to-all-start = ((bf16[3,128,2,1,384]{4,2,0,3,1:T(2,128)(2,1)}), bf16[3,128,2,1,384]{4,2,0,3,1:T(2,128)(2,1)S(1)}, u32[]{:S(2)}, u32[]{:S(2)}) async-start(bf16[3,128,2,1,384]{4,2,0,3,1:T(2,128)(2,1)} %copy.930), calls=%async_computation | async-start | bytes 1179648 | tf_op jit(solution)/shard_map/all_to_all | solution.py:91
  412.6 30.2 %copy-start.1 = (bf16[2,2,384,384]{3,2,1,0:T(8,128)(2,1)S(1)}, bf16[2,2,384,384]{3,2,1,0:T(8,128)(2,1)}, u32[]{:S(2)}) copy-start(bf16[2,2,384,384]{3,2,1,0:T(8,128)(2,1)} %param.8) | copy-start | bytes 3538948
  468.0 24.4 %all-to-all-start.3 = ((bf16[192,2,2,1,384]{4,2,1,3,0:T(2,128)(2,1)}), bf16[192,2,2,1,384]{4,2,1,3,0:T(2,128)(2,1)}, u32[]{:S(2)}, u32[]{:S(2)}) async-start(bf16[192,2,2,1,384]{4,2,1,3,0:T(2,128)(2,1)} %copy.1004), calls=%async_computation.3 | async-start | bytes 1179648 | tf_op jit(solution)/shard_map/all_to_all | solution.py:106
  473.7 126.6 %all-gather.2.cloned.1.call-start = ((), (), s32[]{:S(2)}) async-start(), calls=%async_computation.8 | async-start | bytes 7077888 | tf_op jit(solution)/shard_map/all_gather | solution.py:16
  577.4 20.8 %all-to-all-start.7 = ((bf16[192,2,2,1,384]{4,2,1,3,0:T(2,128)(2,1)}), bf16[192,2,2,1,384]{4,2,1,3,0:T(2,128)(2,1)S(1)}, u32[]{:S(2)}, u32[]{:S(2)}) async-start(bf16[192,2,2,1,384]{4,2,1,3,0:T(2,128)(2,1)} %copy.1078), calls=%async_computation.7 | async-start | bytes 1179648 | tf_op jit(solution)/shard_map/all_to_all | solution.py:106
  582.1 16.8 %copy-start.2 = (bf16[1,3,384,384]{3,2,1,0:T(8,128)(2,1)S(1)}, bf16[1,3,384,384]{3,2,1,0:T(8,128)(2,1)}, u32[]{:S(2)}) copy-start(bf16[1,3,384,384]{3,2,1,0:T(8,128)(2,1)} %param.7) | copy-start | bytes 2654212
  600.3 6.0 copy-start.4
Sparse Core Ops, SparseCore 0:
  553.4 37.0 all-gather.1
